TPU v7x, 1024 devices: a whole 4x4x32 slice. The times are simulated.
1024 devices in a mesh: row: 16 (over y, x), col: 64 (over z, core).
Axes of the slice: x: 4, y: 4, z: 32, core: 2. Of those that a mesh axis runs over, the one named last changes fastest.
Arguments:
- features: float32 [131072, 256], P(('col', 'row')), may hold values from -6 to 6
- weight: float32 [256, 128], replicated, may hold values from -0.375 to 0.375
- bias: float32 [128], replicated, may hold values from -3 to 3
- adjacency_tiles: bfloat16 [16, 64, 16, 128, 128], P('row', 'col'), may hold values from -0.046875 to 0.046875
- tile_index: int32 [16, 64, 16], P('row', 'col'), may hold values from 0 to 1023, as said below
- tile_count: int32 [16, 64], P('row', 'col'), may hold values from 1 to 16, as said below
- cotangent: float32 [131072, 128], P(('row', 'col')), may hold values from -6 to 6
Outputs:
- hidden: float32 [131072, 128], P(('row', 'col'))
- grad_features: float32 [131072, 256], P(('col', 'row'))
- grad_weight: float32 [256, 128], replicated
- grad_bias: float32 [128], replicated
Inputs may be any that keep to these rules, and one draw needn't show every extreme that they name: `tile_index`: the slots of one block name distinct positions. `tile_count`: some block holds 16 live tiles.
All inputs are finite; a program needn't handle non-finite values.
Results may differ from a plain program's by a relative error of at most 0.013.
Values may be sent and summed in bfloat16 or wider, within the bound.
A program may use at most 64 MiB of HBM per device.

v0:
```python
import jax
import jax.numpy as jnp
from jax import lax
from jax.sharding import PartitionSpec as P


def gelu_parts(values):
    normal_cdf = 0.5 * (1.0 + jax.scipy.special.erf(values * 0.7071067811865476))
    density = jnp.exp(-0.5 * values * values) * 0.3989422804014327
    return (values * normal_cdf, normal_cdf + values * density)


def aggregate(pieces, where, live_count, panel_rows, row_tiles, col_tiles):
    highest = lax.Precision.HIGHEST
    slots_total, tile_size = (pieces.shape[0], pieces.shape[1])
    feature_width = panel_rows.shape[1]
    group_size = min(8, slots_total)
    passes = (live_count + group_size - 1) // group_size
    panels = panel_rows.reshape(col_tiles, tile_size, feature_width)
    tile_row_ids = jnp.arange(row_tiles, dtype=jnp.int32)

    def advance(passed, totals):
        first_slot = passed * group_size
        piece_tiles = lax.dynamic_slice_in_dim(pieces, first_slot, group_size, 0).astype(
            jnp.float32
        )
        chosen = lax.dynamic_slice_in_dim(where, first_slot, group_size, 0)
        living = (first_slot + jnp.arange(group_size, dtype=jnp.int32) < live_count).astype(
            jnp.float32
        )
        gathered = panels[chosen % col_tiles].astype(jnp.float32)
        products = (
            jnp.einsum("kij,kjf->kif", piece_tiles, gathered, precision=highest)
            * living[:, None, None]
        )
        onehot = ((chosen // col_tiles)[:, None] == tile_row_ids[None, :]).astype(jnp.float32)
        return totals + jnp.einsum("kr,kif->rif", onehot, products, precision=highest)

    empty = jnp.zeros((row_tiles, tile_size, feature_width), jnp.float32)
    return lax.fori_loop(0, passes, advance, empty).reshape(row_tiles * tile_size, feature_width)


def aggregate_back(pieces, where, live_count, grad_rows, row_tiles, col_tiles):
    highest = lax.Precision.HIGHEST
    slots_total, tile_size = (pieces.shape[0], pieces.shape[1])
    feature_width = grad_rows.shape[1]
    group_size = min(8, slots_total)
    passes = (live_count + group_size - 1) // group_size
    grad_panels = grad_rows.reshape(row_tiles, tile_size, feature_width)
    tile_col_ids = jnp.arange(col_tiles, dtype=jnp.int32)

    def advance(passed, totals):
        first_slot = passed * group_size
        piece_tiles = lax.dynamic_slice_in_dim(pieces, first_slot, group_size, 0).astype(
            jnp.float32
        )
        chosen = lax.dynamic_slice_in_dim(where, first_slot, group_size, 0)
        living = (first_slot + jnp.arange(group_size, dtype=jnp.int32) < live_count).astype(
            jnp.float32
        )
        gathered = grad_panels[chosen // col_tiles].astype(jnp.float32)
        products = (
            jnp.einsum("kji,kjf->kif", piece_tiles, gathered, precision=highest)
            * living[:, None, None]
        )
        onehot = ((chosen % col_tiles)[:, None] == tile_col_ids[None, :]).astype(jnp.float32)
        return totals + jnp.einsum("kc,kif->cif", onehot, products, precision=highest)

    empty = jnp.zeros((col_tiles, tile_size, feature_width), jnp.float32)
    return lax.fori_loop(0, passes, advance, empty).reshape(col_tiles * tile_size, feature_width)


def local(features, weight, bias, adjacency_tiles, tile_index, tile_count, cotangent):
    highest = lax.Precision.HIGHEST
    pieces = adjacency_tiles[0, 0]
    where = tile_index[0, 0]
    live_count = tile_count[0, 0]
    rows_dev = features.shape[0]
    tile_size = pieces.shape[1]
    row_count = lax.axis_size("row")
    col_count = lax.axis_size("col")
    col_tiles = rows_dev * row_count // tile_size
    row_tiles = rows_dev * col_count // tile_size
    product = jnp.dot(features, weight, precision=highest, preferred_element_type=jnp.float32)
    panel_rows = lax.all_gather(product.astype(jnp.bfloat16), "row", axis=0, tiled=True)
    partial_value = aggregate(pieces, where, live_count, panel_rows, row_tiles, col_tiles)
    aggregated = lax.psum_scatter(partial_value, "col", scatter_dimension=0, tiled=True)
    preact = aggregated + bias
    hidden, slopes = gelu_parts(preact)
    grad_preact = cotangent * slopes
    grad_rows = lax.all_gather(grad_preact.astype(jnp.bfloat16), "col", axis=0, tiled=True)
    back_partial = aggregate_back(pieces, where, live_count, grad_rows, row_tiles, col_tiles)
    grad_product = lax.psum_scatter(
        back_partial.astype(jnp.bfloat16), "row", scatter_dimension=0, tiled=True
    ).astype(jnp.float32)
    grad_features = jnp.dot(
        grad_product, weight.T, precision=highest, preferred_element_type=jnp.float32
    )
    weight_term = jnp.dot(
        features.T, grad_product, precision=highest, preferred_element_type=jnp.float32
    )
    bias_term = jnp.sum(grad_preact, axis=0)
    weight_total, bias_total = lax.psum((weight_term, bias_term), ("row", "col"))
    scaling = 1.0 / jnp.sqrt(jnp.float32(rows_dev * row_count * col_count))
    return (hidden, grad_features, weight_total * scaling, bias_total * scaling)


def solution(mesh):
    placed = (
        P(("col", "row"), None),
        P(),
        P(),
        P("row", "col", None, None, None),
        P("row", "col", None),
        P("row", "col"),
        P(("row", "col"), None),
    )
    return jax.shard_map(
        local,
        mesh=mesh,
        in_specs=placed,
        out_specs=(P(("row", "col"), None), P(("col", "row"), None), P(), P()),
        check_vma=False,
    )
```

profile of v0, /device:TPU:1, one launch (start us, length us, event | category | flops | bytes accessed | tf_op | source)
XLA Modules:
  0.0 1430.8 jit_solution(16396817230468305843)
XLA Ops:
  7.2 0.0 copy-start
  7.2 0.0 copy-start.3
  7.2 0.0 copy-start.1
  7.2 0.0 reduce-scatter.3.cloned.1.call-start
  8.0 0.1 copy-done
  8.1 1.2 convolution_convert_fusion
  9.3 20.0 %all_gather.6 = bf16[2048,128]{1,0:T(8,128)(2,1)S(1)} all-gather(bf16[128,128]{1,0:T(8,128)(2,1)S(1)} %convolution_convert_fusion), channel_id=1, replica_groups=mesh['row'=16,'col'=64] {'row'}, dimensions={0}, use_global_device_ids=true | all-gather | bytes 557056 | tf_op jit(solution)/shard_map/all_gather | solution.py:85
  29.2 2.5 broadcast_in_dim.25
  31.7 0.0 copy-done.3
  31.7 0.0 copy-done.1
  31.7 7.7 while.26
  31.7 0.1 and_select_fusion.6
  31.8 0.6 gather_fusion
  32.4 0.2 fusion.45
  32.7 0.7 compare_convert_fusion.4
  33.3 6.1 convolution_add_fusion.4
  39.4 6.6 copy.13
  46.0 0.0 copy-start.4
  46.0 0.0 reduce-scatter.3.cloned.1.call-update
  46.0 0.0 all-gather.2.cloned.1.call-start
  46.0 229.9 %reduce-scatter.3.cloned.1.call-done = f32[128,128]{1,0:T(8,128)} async-done(((f32[8192,128]{1,0:T(8,128)}), f32[128,128]{1,0:T(8,128)}) %reduce-scatter.3.cloned.1.call-update) | async-done | bytes 65552 | tf_op jit(solution)/shard_map/reduce_scatter | solution.py:87
  276.0 0.0 copy-done.4
  276.0 0.0 copy-done.5
  276.0 1.5 fusion.23
  277.5 0.0 all-gather.2.cloned.1.call-update
  277.5 0.0 reduce-scatter.5.cloned.1.call-start
  277.6 138.6 %all-gather.2.cloned.1.call-done = bf16[8192,128]{1,0:T(8,128)(2,1)} async-done(((bf16[128,128]{1,0:T(8,128)(2,1)}), bf16[8192,128]{1,0:T(8,128)(2,1)}) %all-gather.2.cloned.1.call-update) | async-done | bytes 2097168 | tf_op jit(solution)/shard_map/all_gather | solution.py:91
  416.1 0.1 broadcast_in_dim.26
  416.2 0.0 copy-start.2
  416.2 4.4 while.27
  416.3 0.1 and_select_fusion.7
  416.3 0.1 compare_select_fusion.13
  416.4 2.2 gather_fusion.1
  418.6 0.3 fusion.49
  418.9 0.7 compare_convert_fusion.5
  419.6 1.1 convolution_add_fusion.5
  420.7 1.1 copy.23
  421.8 0.0 reduce-scatter.5.cloned.1.call-update
  421.8 0.0 all-reduce.2.cloned.1.call-start
  421.9 157.2 %psum.15 = f32[128]{0:T(128)S(1)} all-reduce(f32[128]{0:T(128)S(1)} %get-tuple-element.294), channel_id=1, replica_groups=mesh['row'=16,'col'=64] {'row','col'}, use_global_device_ids=true, to_apply=%region_8.9 | all-reduce | flops 128 | bytes 1024 | tf_op jit(solution)/shard_map/psum | solution.py:103
  579.1 0.5 broadcast_multiply_fusion.1
  579.6 1.7 convolution_bitcast_fusion
  581.3 0.0 all-reduce.2.cloned.1.call-update
  581.4 0.0 copy-done.2
  581.4 1.6 fusion.25
  583.0 839.6 %all-reduce.2.cloned.1.call-done = f32[256,128]{0,1:T(8,128)} async-done(((f32[256,128]{0,1:T(8,128)}), f32[256,128]{0,1:T(8,128)}) %all-reduce.2.cloned.1.call-update) | async-done | bytes 131088 | tf_op jit(solution)/shard_map/psum | solution.py:103
  1422.6 0.9 broadcast_multiply_fusion
  1423.5 0.8 copy.15
  (5 shorter events, 0.0 us)
Async XLA Ops:
  7.2 0.9 copy-start
  7.2 24.5 %copy-start.3 = (s32[1,1,16]{2,1,0:T(1,128)S(1)}, s32[1,1,16]{2,1,0:T(1,128)}, u32[]{:S(2)}) copy-start(s32[1,1,16]{2,1,0:T(1,128)} %param.15) | copy-start | bytes 196
  7.2 24.5 %copy-start.1 = (bf16[1,1,16,128,128]{4,3,2,1,0:T(8,128)(2,1)S(1)}, bf16[1,1,16,128,128]{4,3,2,1,0:T(8,128)(2,1)}, u32[]{:S(2)}) copy-start(bf16[1,1,16,128,128]{4,3,2,1,0:T(8,128)(2,1)} %param.14) | copy-start | bytes 1572868
  7.2 268.8 %reduce-scatter.3.cloned.1.call-start = ((), (), s32[]{:S(2)}) async-start(), calls=%async_computation.2 | async-start | bytes 4259840 | tf_op jit(solution)/shard_map/reduce_scatter | solution.py:87
  46.0 230.0 %copy-start.4 = (f32[128,128]{1,0:T(8,128)S(1)}, f32[128,128]{1,0:T(8,128)}, u32[]{:S(2)}) copy-start(f32[128,128]{1,0:T(8,128)} %param.17) | copy-start | bytes 196612
  46.0 230.0 %copy-start.5 = (f32[128]{0:T(128)S(1)}, f32[128]{0:T(128)}, u32[]{:S(2)}) copy-start(f32[128]{0:T(128)} %param.13) | copy-start | bytes 1540
  46.0 370.2 %all-gather.2.cloned.1.call-start = ((), (), s32[]{:S(2)}) async-start(), calls=%async_computation.3 | async-start | bytes 2129920 | tf_op jit(solution)/shard_map/all_gather | solution.py:91
  277.5 302.1 %reduce-scatter.5.cloned.1.call-start = ((), (), s32[]{:S(2)}) async-start(), calls=%async_computation.4 | async-start | bytes 557056 | tf_op jit(solution)/shard_map/reduce_scatter | solution.py:93
  416.2 165.1 %copy-start.2 = (f32[256,128]{1,0:T(8,128)S(1)}, f32[256,128]{1,0:T(8,128)}, u32[]{:S(2)}) copy-start(f32[256,128]{1,0:T(8,128)} %param.12) | copy-start | bytes 393220
  421.8 1000.8 %all-reduce.2.cloned.1.call-start = ((), (), s32[]{:S(2)}) async-start(), calls=%async_computation.5 | async-start | bytes 262144 | tf_op jit(solution)/shard_map/psum | solution.py:103
Sparse Core Ops, SparseCore 0:
  46.1 229.8 reduce-scatter.2
  279.6 136.4 all-gather.1
  422.2 101.0 reduce-scatter.4
  581.5 841.0 all-reduce.1
where the time goes:
time: 1430 us
  waiting for transfers between devices  1210 us (85%)
  blocking collectives  177 us (12%)
  between operations  14.6 us (1%)
    psum x1, waiting for transfers between devices, local(): lax.psum((weight_term, bias_term), ('row', 'col'))  840 us
    reduce_scatter x1, waiting for transfers between devices, local(): lax.psum_scatter(partial_value, 'col', scatter_dimension=0, tiled=True)  230 us
    psum x1, blocking collectives, local(): lax.psum((weight_term, bias_term), ('row', 'col'))  157 us
    all_gather x1, waiting for transfers between devices, local(): lax.all_gather(grad_preact.astype(jnp.bfloat16), 'col', axis=0, tiled=True)  139 us
  transfers between devices with their start and end apart: 4, of which 3 were waited for; matrix products, arithmetic and copies ran while one was open for 0% of the time, Pallas kernels for 0%

commit v1 on v0

v1 whole, which is shorter than its diff:
```python
import functools
import math

import jax
import jax.numpy as jnp
from jax import lax
from jax.experimental import pallas as pl
from jax.experimental.pallas import tpu as pltpu
from jax.sharding import PartitionSpec as P

F32, BF16 = jnp.float32, jnp.bfloat16
HIGHEST = lax.Precision.HIGHEST


def gelu_parts(values):
    normal_cdf = 0.5 * (1.0 + lax.erf(values * 0.7071067811865476))
    density = jnp.exp(-0.5 * values * values) * 0.3989422804014327
    return (values * normal_cdf, normal_cdf + values * density)


def layer(
    n_row,
    nz,
    scaling,
    where,
    live,
    features,
    weight,
    bias,
    cotangent,
    tiles_hbm,
    hidden_out,
    grad_features_out,
    grad_weight_out,
    grad_bias_out,
    tiles,
    tiles_t,
    features_t,
    panel,
    products,
    compact,
    to_sib,
    from_sib,
    up,
    down,
    grads,
    back,
    back_in,
    terms,
    terms_in,
    near,
    far,
    total,
    prev_row,
    prev_col,
    last_row,
    last_col,
    tile_sem,
    panel_send,
    panel_recv,
    sib_send,
    sib_recv,
    up_send,
    up_recv,
    down_send,
    down_recv,
    right_send,
    right_recv,
    left_send,
    left_recv,
    pass_send,
    pass_recv,
    back_send,
    back_recv,
    terms_send,
    terms_recv,
    near_send,
    near_recv,
    far_send,
    far_recv,
    total_send,
    total_recv,
):
    slots = tiles.shape[0]
    row, col = lax.axis_index("row"), lax.axis_index("col")
    z, core = col // 2, col % 2
    half = nz // 2
    near_n = math.gcd(8, nz) if nz >= 16 else 2
    far_n = nz // near_n
    n_plane = 2 * n_row
    place = 2 * row + core
    group, spot = z // near_n, z % near_n

    def device(at_row, at_z, at_core):
        return (at_row, 2 * at_z + at_core)

    def remote(src, dst, send, recv, to):
        return pltpu.make_async_remote_copy(
            src_ref=src,
            dst_ref=dst,
            send_sem=send,
            recv_sem=recv,
            device_id=to,
            device_id_type=pl.DeviceIdType.MESH,
        )

    def settle(ref, sem):
        pltpu.make_async_copy(ref, ref, sem).wait()

    right = device(row, (z + 1) % nz, core)
    left = device(row, (z + nz - 1) % nz, core)
    sibling = device(row, z, 1 - core)

    def plane(step):
        other = (place + step) % n_plane
        return device(other // 2, z, other % 2), other

    def near_peer(step):
        return device(row, group * near_n + (spot + step) % near_n, core)

    def far_peer(step):
        return device(row, (z + near_n * step) % nz, core)

    barrier = pltpu.get_barrier_semaphore()

    def greet(to):
        pl.semaphore_signal(
            barrier, inc=1, device_id=to, device_id_type=pl.DeviceIdType.MESH
        )

    @pl.loop(1, n_plane)
    def _(step):
        greet(plane(step)[0])

    @pl.loop(1, near_n)
    def _(step):
        greet(near_peer(step))

    @pl.loop(1, far_n)
    def _(step):
        greet(far_peer(step))

    greet(right)
    greet(left)

    tile_copy = pltpu.make_async_copy(tiles_hbm, tiles, tile_sem)
    tile_copy.start()
    panel[row] = jnp.dot(
        features[...], weight[...], precision=HIGHEST, preferred_element_type=F32
    ).astype(BF16)
    pl.semaphore_wait(barrier, n_plane - 1 + near_n - 1 + far_n - 1 + 2)

    def panel_copy(step):
        return remote(
            panel.at[row],
            panel.at[row],
            panel_send.at[step],
            panel_recv.at[step],
            device((row + step) % n_row, z, core),
        )

    @pl.loop(1, n_row)
    def _(step):
        panel_copy(step).start()

    count = live[0]
    n_cols = n_row

    @pl.loop(0, slots)
    def _(slot):
        mine = where[slot]
        by_row, by_col = jnp.int32(slots), jnp.int32(slots)
        for other in range(slots):
            theirs = where[other]
            before = other < slot
            by_row = jnp.where(
                before & (theirs // n_cols == mine // n_cols), other, by_row
            )
            by_col = jnp.where(
                before & (theirs % n_cols == mine % n_cols), other, by_col
            )
        prev_row[slot] = by_row
        prev_col[slot] = by_col

    @pl.loop(0, 2 * nz)
    def _(tile_row):
        last = jnp.int32(slots)
        for other in range(slots):
            last = jnp.where(
                (other < count) & (where[other] // n_cols == tile_row), other, last
            )
        last_row[tile_row] = last

    @pl.loop(0, n_cols)
    def _(tile_col):
        last = jnp.int32(slots)
        for other in range(slots):
            last = jnp.where(
                (other < count) & (where[other] % n_cols == tile_col), other, last
            )
        last_col[tile_col] = last

    products[slots] = jnp.zeros_like(products[slots])
    compact[slots] = jnp.zeros_like(compact[slots])
    tile_copy.wait()

    @pl.loop(1, n_row)
    def _(step):
        panel_copy(step).wait_recv()

    for slot in range(slots):
        products[slot] = jnp.dot(
            tiles[slot], panel[where[slot] % n_cols], preferred_element_type=F32
        )

    @pl.loop(0, slots)
    def _(slot):
        added = products[slot] + products[prev_row[slot]]
        products[slot] = added
        compact[slot] = added.astype(BF16)

    parts = sib_send.shape[0] // 2
    width = half // parts

    def sib_copies(part):
        for end, first in enumerate((part * width, nz - width - part * width)):
            yield remote(
                to_sib.at[pl.ds(first, width)],
                from_sib.at[pl.ds(first, width)],
                sib_send.at[2 * part + end],
                sib_recv.at[2 * part + end],
                sibling,
            )

    def slot_of(at, whose):
        return last_row[2 * ((z + at + nz - (half - 1)) % nz) + whose]

    for part in range(parts):

        @pl.loop(part * width, (part + 1) * width)
        def _(at):
            to_sib[at] = compact[slot_of(at, 1 - core)]
            to_sib[nz - 1 - at] = compact[slot_of(nz - 1 - at, 1 - core)]

        for copy in sib_copies(part):
            copy.start()

    def up_copy(step):
        return remote(up.at[step], up.at[step + 1], up_send, up_recv.at[step], right)

    def down_copy(step):
        return remote(
            down.at[step], down.at[step + 1], down_send, down_recv.at[step], left
        )

    def chip_part(at):
        return compact[slot_of(at, core)].astype(F32) + from_sib[at].astype(F32)

    for part in range(parts):
        for copy in sib_copies(part):
            copy.wait_recv()
        if part == 0:
            up[0] = chip_part(nz - 1).astype(BF16)
            up_copy(0).start()
            down[0] = chip_part(0).astype(BF16)
            down_copy(0).start()

        @pl.loop(max(1, part * width), (part + 1) * width)
        def _(step):
            mine = chip_part(nz - 1 - step)
            up_copy(step - 1).wait_recv()
            up[step] = (up[step].astype(F32) + mine).astype(BF16)
            up_copy(step).start()

            @pl.when(step < half - 1)
            def _():
                mine = chip_part(step)
                down_copy(step - 1).wait_recv()
                down[step] = (down[step].astype(F32) + mine).astype(BF16)
                down_copy(step).start()

    own = products[slot_of(half - 1, core)] + from_sib[half - 1].astype(F32)
    own = own + bias[...]
    down_copy(half - 2).wait_recv()
    own = own + down[half - 1].astype(F32)
    up_copy(half - 1).wait_recv()
    preact = own + up[half].astype(F32)
    hidden, slopes = gelu_parts(preact)
    grad_preact = cotangent[...] * slopes
    grads[core, z] = grad_preact.astype(BF16)

    def right_copy(step):
        at = grads.at[core, (z + nz - step) % nz]
        return remote(at, at, right_send, right_recv.at[step], right)

    def left_copy(step):
        at = grads.at[core, (z + step) % nz]
        return remote(at, at, left_send, left_recv.at[step], left)

    def pass_copy(at_z):
        at = grads.at[core, at_z]
        return remote(at, at, pass_send, pass_recv, sibling)

    right_copy(0).start()
    left_copy(0).start()
    pass_copy(z).start()
    hidden_out[...] = hidden
    rows_dev, width_out = grad_preact.shape
    bias_term = jnp.sum(grad_preact.reshape(rows_dev // 8, 8, width_out), axis=0)

    @pl.loop(0, n_plane)
    def _(at):
        terms[at, 8:16] = bias_term

    @pl.loop(0, slots)
    def _(slot):
        tiles_t[slot] = tiles[slot].T

    features_t[...] = features[...].T


    @pl.loop(0, half)
    def _(step):
        from_left = (z + nz - 1 - step) % nz
        right_copy(step).wait_recv()

        @pl.when(step < half - 1)
        def _():
            right_copy(step + 1).start()

        pass_copy(from_left).start()

        @pl.when(step < half - 1)
        def _():
            from_right = (z + 1 + step) % nz
            left_copy(step).wait_recv()

            @pl.when(step < half - 2)
            def _():
                left_copy(step + 1).start()

            pass_copy(from_right).start()

    settle(grads.at[1 - core], pass_recv)

    for slot in range(slots):
        tile_row = where[slot] // n_cols
        products[slot] = jnp.dot(
            tiles_t[slot],
            grads[tile_row % 2, tile_row // 2],
            preferred_element_type=F32,
        )

    @pl.loop(0, slots)
    def _(slot):
        products[slot] = products[slot] + products[prev_col[slot]]

    def back_copy(step):
        to = (row + step) % n_row
        return remote(
            back.at[step],
            back_in.at[step],
            back_send.at[step],
            back_recv.at[step],
            device(to, z, core),
        )

    @pl.loop(1, n_row)
    def _(step):
        back[step] = products[last_col[(row + step) % n_row]].astype(BF16)
        back_copy(step).start()

    products[slots] = products[last_col[row]].astype(BF16).astype(F32)

    @pl.loop(1, n_row)
    def _(step):
        back_copy(step).wait_recv()
        products[slots] = products[slots] + back_in[step].astype(F32)

    grad_product = products[slots]

    weight_term = jnp.dot(
        features_t[...], grad_product, precision=HIGHEST, preferred_element_type=F32
    )
    for at in range(n_plane):
        terms[at, 0:8] = weight_term[8 * at : 8 * at + 8]

    def terms_copy(step):
        to, other = plane(step)
        return remote(
            terms.at[other],
            terms_in.at[place],
            terms_send.at[step],
            terms_recv.at[step],
            to,
        )

    @pl.loop(1, n_plane)
    def _(step):
        terms_copy(step).start()

    grad_features_out[...] = lax.dot_general(
        grad_product,
        weight[...],
        (((1,), (1,)), ((), ())),
        precision=HIGHEST,
        preferred_element_type=F32,
    )
    terms_in[place] = terms[place]

    @pl.loop(1, n_plane)
    def _(step):
        terms_copy(step).wait_recv()

    near[spot] = lax.fori_loop(
        1, n_plane, lambda at, so_far: so_far + terms_in[at], terms_in[0]
    )

    def near_copy(step):
        return remote(
            near.at[spot],
            near.at[spot],
            near_send.at[step],
            near_recv.at[step],
            near_peer(step),
        )

    def far_copy(step):
        return remote(
            far.at[group],
            far.at[group],
            far_send.at[step],
            far_recv.at[step],
            far_peer(step),
        )

    for step in range(1, near_n):
        near_copy(step).start()
    for step in range(1, near_n):
        near_copy(step).wait_recv()
    far[group] = sum((near[at] for at in range(1, near_n)), near[0])
    for step in range(1, far_n):
        far_copy(step).start()
    for step in range(1, far_n):
        far_copy(step).wait_recv()
    summed = sum((far[at] for at in range(1, far_n)), far[0]) * scaling
    total[place] = summed[0:8]

    def total_copy(step):
        return remote(
            total.at[place],
            total.at[place],
            total_send.at[step],
            total_recv.at[step],
            plane(step)[0],
        )

    @pl.loop(1, n_plane)
    def _(step):
        total_copy(step).start()

    grad_bias_out[...] = jnp.sum(summed[8:16], axis=0, keepdims=True)

    @pl.loop(1, n_row)
    def _(step):
        panel_copy(step).wait_send()
        back_copy(step).wait_send()

    for part in range(parts):
        for copy in sib_copies(part):
            copy.wait_send()
    settle(up.at[pl.ds(0, half)], up_send)
    settle(down.at[pl.ds(0, half - 1)], down_send)
    settle(grads.at[0, pl.ds(0, half)], right_send)
    settle(grads.at[0, pl.ds(0, half - 1)], left_send)
    settle(grads.at[0], pass_send)

    @pl.loop(1, n_plane)
    def _(step):
        terms_copy(step).wait_send()

    for step in range(1, near_n):
        near_copy(step).wait_send()
    for step in range(1, far_n):
        far_copy(step).wait_send()

    @pl.loop(1, n_plane)
    def _(step):
        total_copy(step).wait_recv()

    grad_weight_out[...] = total[...]

    @pl.loop(1, n_plane)
    def _(step):
        total_copy(step).wait_send()


def local(n_row, n_col, features, weight, bias, tiles, where, live, cotangent):
    slots, tile = tiles.shape[2], tiles.shape[3]
    rows_dev, f_in = features.shape
    f_out = weight.shape[1]
    nz = n_col // 2
    half = nz // 2
    near_n = math.gcd(8, nz) if nz >= 16 else 2
    far_n = nz // near_n
    n_plane = 2 * n_row
    parts = min(4, half)
    nodes = rows_dev * n_row * n_col
    chunk = f_in // n_plane
    assert chunk == 8 and rows_dev == tile
    dma = pltpu.SemaphoreType.DMA
    vmem = pl.BlockSpec(memory_space=pltpu.VMEM)
    smem = pl.BlockSpec(memory_space=pltpu.SMEM)
    hidden, grad_features, grad_weight, grad_bias = pl.pallas_call(
        functools.partial(layer, n_row, nz, 1.0 / math.sqrt(nodes)),
        out_shape=(
            jax.ShapeDtypeStruct((rows_dev, f_out), F32),
            jax.ShapeDtypeStruct((rows_dev, f_in), F32),
            jax.ShapeDtypeStruct((n_plane, chunk, f_out), F32),
            jax.ShapeDtypeStruct((1, f_out), F32),
        ),
        in_specs=[smem, smem, vmem, vmem, vmem, vmem, pl.BlockSpec(memory_space=pl.ANY)],
        out_specs=(vmem, vmem, vmem, vmem),
        scratch_shapes=[
            pltpu.VMEM((slots, tile, tile), BF16),
            pltpu.VMEM((slots, tile, tile), BF16),
            pltpu.VMEM((f_in, rows_dev), F32),
            pltpu.VMEM((n_row, tile, f_out), BF16),
            pltpu.VMEM((slots + 1, tile, f_out), F32),
            pltpu.VMEM((slots + 1, tile, f_out), BF16),
            pltpu.VMEM((nz, tile, f_out), BF16),
            pltpu.VMEM((nz, tile, f_out), BF16),
            pltpu.VMEM((half + 1, tile, f_out), BF16),
            pltpu.VMEM((half, tile, f_out), BF16),
            pltpu.VMEM((2, nz, tile, f_out), BF16),
            pltpu.VMEM((n_row, tile, f_out), BF16),
            pltpu.VMEM((n_row, tile, f_out), BF16),
            pltpu.VMEM((n_plane, 2 * chunk, f_out), F32),
            pltpu.VMEM((n_plane, 2 * chunk, f_out), F32),
            pltpu.VMEM((near_n, 2 * chunk, f_out), F32),
            pltpu.VMEM((far_n, 2 * chunk, f_out), F32),
            pltpu.VMEM((n_plane, chunk, f_out), F32),
            pltpu.SMEM((slots,), jnp.int32),
            pltpu.SMEM((slots,), jnp.int32),
            pltpu.SMEM((n_col,), jnp.int32),
            pltpu.SMEM((n_row,), jnp.int32),
            dma,
            dma((n_row,)),
            dma((n_row,)),
            dma((2 * parts,)),
            dma((2 * parts,)),
            dma,
            dma((half,)),
            dma,
            dma((half,)),
            dma,
            dma((half,)),
            dma,
            dma((half,)),
            dma,
            dma,
            dma((n_row,)),
            dma((n_row,)),
            dma((n_plane,)),
            dma((n_plane,)),
            dma((near_n,)),
            dma((near_n,)),
            dma((far_n,)),
            dma((far_n,)),
            dma((n_plane,)),
            dma((n_plane,)),
        ],
        compiler_params=pltpu.CompilerParams(
            collective_id=0, has_side_effects=True, vmem_limit_bytes=48 * 1024 * 1024
        ),
    )(
        where.reshape(slots),
        live.reshape(1),
        features,
        weight,
        bias.reshape(1, f_out),
        cotangent,
        tiles.reshape(slots, tile, tile),
    )
    return (
        hidden,
        grad_features,
        grad_weight.reshape(f_in, f_out),
        grad_bias.reshape(f_out),
    )


def solution(mesh):
    placed = (
        P(("col", "row"), None),
        P(),
        P(),
        P("row", "col", None, None, None),
        P("row", "col", None),
        P("row", "col"),
        P(("row", "col"), None),
    )
    return jax.shard_map(
        functools.partial(local, mesh.shape["row"], mesh.shape["col"]),
        mesh=mesh,
        in_specs=placed,
        out_specs=(P(("row", "col"), None), P(("col", "row"), None), P(), P()),
        check_vma=False,
    )
```

time: 1430 us -> 191 us (0.13)
  waiting for transfers between devices: 1210 us -> 0 us
  Pallas kernels: 0 us -> 182 us
  blocking collectives: 177 us -> 0 us
    psum x1 -> x0, waiting for transfers between devices: 840 us -> none  [local(): lax.psum((weight_term, bias_term), ('row', 'col'))]
    reduce_scatter x2 -> x0, waiting for transfers between devices: 230 us -> none  [the longest x1 230 us: local(): lax.psum_scatter(partial_value, 'col', scatter_dimension=0, tiled=True)]
    pallas_call x0 -> x1, Pallas kernels: none -> 182 us  [local(): pl.pallas_call(functools.partial(layer, n_row, nz, 1.0 / math.sqrt(nodes)...]
    psum x1 -> x0, blocking collectives: 157 us -> none  [local(): lax.psum((weight_term, bias_term), ('row', 'col'))]
    all_gather x1 -> x0, waiting for transfers between devices: 139 us -> none  [local(): lax.all_gather(grad_preact.astype(jnp.bfloat16), 'col', axis=0, tiled=True)]
    all_gather x1 -> x0, blocking collectives: 20 us -> none  [local(): lax.all_gather(product.astype(jnp.bfloat16), 'row', axis=0, tiled=True)]
  transfers between devices with their start and end apart: 4 -> 0, of which waited for: 3 -> 0; matrix products, arithmetic and copies ran while one was open for 0% -> 0% of each run, Pallas kernels for 0% -> 0%
where the time goes in v1:
time: 191 us; the launch traced here: 190 us
  Pallas kernels  182 us (95%)
  local copies, waits for them, and re-layouts  6.8 us (4%)
    pallas_call x1, Pallas kernels, local(): pl.pallas_call(functools.partial(layer, n_row, nz, 1.0 / math.sqrt(nodes)...  182 us
    unnamed x16, local copies, waits for them, and re-layouts  6.8 us

profile of v1, /device:TPU:1, one launch (start us, length us, event | category | flops | bytes accessed | tf_op | source)
XLA Modules:
  0.0 190.3 jit_solution(16459991886656893322)
XLA Ops:
  1.3 0.0 copy-start.4
  1.3 0.0 copy-start.5
  1.3 0.6 copy-done.4
  1.9 0.0 copy-done.5
  2.0 0.0 copy-start
  2.0 1.0 copy-done
  3.0 0.0 copy-start.1
  3.0 0.9 copy-done.1
  3.9 0.0 copy-start.2
  3.9 0.9 copy-done.2
  4.8 0.0 copy-start.3
  4.8 0.8 copy-done.3
  5.6 182.2 %shard_map.102 = (f32[128,128]{1,0:T(8,128)S(1)}, f32[128,256]{1,0:T(8,128)S(1)}, f32[32,8,128]{2,1,0:T(8,128)S(1)}, f32[1,128]{1,0:T(1,128)S(1)}) custom-call(s32[16]{0:T(128)S(1)} %bitcast.9, s32[1]{0:T(128)} %bitcast.6.live, f32[128,256]{1,0:T(8,128)S(1)} %copy-done.1, f32[256,128]{1,0:T(8,128)S(1)} %copy-done.2, f32[1,128]{1,0:T(1,128)S(1)} %bitcast.10, ...), custom_call_target="tpu_custom_call" | custom-call | tf_op jit(solution)/shard_map/pallas_call | solution.py:514
  187.8 0.6 copy.16
  188.5 0.7 copy.17
  189.1 0.7 copy.18
  189.8 0.5 copy.19
Async XLA Ops:
  1.3 0.7 copy-start.4
  1.3 0.7 copy-start.5
  2.0 1.0 copy-start
  3.0 0.9 copy-start.1
  3.9 0.9 copy-start.2
  4.8 0.8 copy-start.3

commit v2 on v1

--- a/solution.py
+++ b/solution.py
@@ -12,6 +12,13 @@
 HIGHEST = lax.Precision.HIGHEST
 
 
+def plan(nz):
+    half = nz // 2
+    stride = 4 if half % 4 == 0 and half > 4 else 2
+    near_n = 8 if nz % 8 == 0 and nz > 8 else 2
+    return half, stride, half // stride, near_n, nz // near_n
+
+
 def gelu_parts(values):
     normal_cdf = 0.5 * (1.0 + lax.erf(values * 0.7071067811865476))
     density = jnp.exp(-0.5 * values * values) * 0.3989422804014327
@@ -24,15 +31,19 @@
     scaling,
     where,
     live,
-    features,
-    weight,
-    bias,
-    cotangent,
+    features_hbm,
+    weight_hbm,
+    bias_hbm,
+    cotangent_hbm,
     tiles_hbm,
     hidden_out,
     grad_features_out,
     grad_weight_out,
     grad_bias_out,
+    features,
+    weight,
+    bias,
+    cotangent,
     tiles,
     tiles_t,
     features_t,
@@ -43,6 +54,8 @@
     from_sib,
     up,
     down,
+    up_in,
+    down_in,
     grads,
     back,
     back_in,
@@ -55,7 +68,7 @@
     prev_col,
     last_row,
     last_col,
-    tile_sem,
+    load_sem,
     panel_send,
     panel_recv,
     sib_send,
@@ -84,9 +97,7 @@
     slots = tiles.shape[0]
     row, col = lax.axis_index("row"), lax.axis_index("col")
     z, core = col // 2, col % 2
-    half = nz // 2
-    near_n = math.gcd(8, nz) if nz >= 16 else 2
-    far_n = nz // near_n
+    half, stride, levels, near_n, far_n = plan(nz)
     n_plane = 2 * n_row
     place = 2 * row + core
     group, spot = z // near_n, z % near_n
@@ -107,8 +118,12 @@
     def settle(ref, sem):
         pltpu.make_async_copy(ref, ref, sem).wait()
 
-    right = device(row, (z + 1) % nz, core)
-    left = device(row, (z + nz - 1) % nz, core)
+    def above(hop):
+        return device(row, (z + hop) % nz, core)
+
+    def below(hop):
+        return device(row, (z + nz - hop) % nz, core)
+
     sibling = device(row, z, 1 - core)
 
     def plane(step):
@@ -128,27 +143,34 @@
             barrier, inc=1, device_id=to, device_id_type=pl.DeviceIdType.MESH
         )
 
+    for hop in range(1, stride + 1):
+        greet(above(hop))
+        greet(below(hop))
+
     @pl.loop(1, n_plane)
     def _(step):
         greet(plane(step)[0])
 
-    @pl.loop(1, near_n)
-    def _(step):
-        greet(near_peer(step))
-
-    @pl.loop(1, far_n)
-    def _(step):
-        greet(far_peer(step))
-
-    greet(right)
-    greet(left)
-
-    tile_copy = pltpu.make_async_copy(tiles_hbm, tiles, tile_sem)
-    tile_copy.start()
+    loads = [
+        pltpu.make_async_copy(src, dst, load_sem.at[at])
+        for at, (src, dst) in enumerate(
+            (
+                (features_hbm, features),
+                (weight_hbm, weight),
+                (tiles_hbm, tiles),
+                (bias_hbm, bias),
+                (cotangent_hbm, cotangent),
+            )
+        )
+    ]
+    for load in loads:
+        load.start()
+    loads[0].wait()
+    loads[1].wait()
     panel[row] = jnp.dot(
         features[...], weight[...], precision=HIGHEST, preferred_element_type=F32
     ).astype(BF16)
-    pl.semaphore_wait(barrier, n_plane - 1 + near_n - 1 + far_n - 1 + 2)
+    pl.semaphore_wait(barrier, n_plane - 1 + 2 * stride)
 
     def panel_copy(step):
         return remote(
@@ -202,7 +224,8 @@
 
     products[slots] = jnp.zeros_like(products[slots])
     compact[slots] = jnp.zeros_like(compact[slots])
-    tile_copy.wait()
+    for load in loads[2:]:
+        load.wait()
 
     @pl.loop(1, n_row)
     def _(step):
@@ -219,8 +242,7 @@
         products[slot] = added
         compact[slot] = added.astype(BF16)
 
-    parts = sib_send.shape[0] // 2
-    width = half // parts
+    parts, width = levels, stride
 
     def sib_copies(part):
         for end, first in enumerate((part * width, nz - width - part * width)):
@@ -245,64 +267,92 @@
         for copy in sib_copies(part):
             copy.start()
 
-    def up_copy(step):
-        return remote(up.at[step], up.at[step + 1], up_send, up_recv.at[step], right)
-
-    def down_copy(step):
+    def up_copy(dist):
+        to = above(dist % stride or stride)
+        return remote(up.at[dist], up_in.at[dist], up_send, up_recv.at[dist], to)
+
+    def down_copy(dist):
+        to = below(dist % stride or stride)
         return remote(
-            down.at[step], down.at[step + 1], down_send, down_recv.at[step], left
-        )
-
-    def chip_part(at):
+            down.at[dist], down_in.at[dist], down_send, down_recv.at[dist], to
+        )
+
+    def chip_part(dist):
+        at = half - 1 + dist
         return compact[slot_of(at, core)].astype(F32) + from_sib[at].astype(F32)
 
-    for part in range(parts):
-        for copy in sib_copies(part):
+    def send_up(dist, value):
+        up[dist] = value.astype(BF16)
+        up_copy(dist).start()
+
+    def send_down(dist, value):
+        down[dist] = value.astype(BF16)
+        down_copy(dist).start()
+
+    def fill(level):
+        for copy in sib_copies(levels - 1 - level):
             copy.wait_recv()
-        if part == 0:
-            up[0] = chip_part(nz - 1).astype(BF16)
-            up_copy(0).start()
-            down[0] = chip_part(0).astype(BF16)
-            down_copy(0).start()
-
-        @pl.loop(max(1, part * width), (part + 1) * width)
-        def _(step):
-            mine = chip_part(nz - 1 - step)
-            up_copy(step - 1).wait_recv()
-            up[step] = (up[step].astype(F32) + mine).astype(BF16)
-            up_copy(step).start()
-
-            @pl.when(step < half - 1)
-            def _():
-                mine = chip_part(step)
-                down_copy(step - 1).wait_recv()
-                down[step] = (down[step].astype(F32) + mine).astype(BF16)
-                down_copy(step).start()
+        if level == levels - 1:
+            send_up(half, chip_part(half))
+        for hop in range(stride - 1, 0, -1):
+            dist = level * stride + hop
+            send_down(dist, chip_part(-dist))
+            send_up(dist, chip_part(dist))
+
+    def gather_up(level, value):
+        for dist in range(level * stride + 1, (level + 1) * stride + 1):
+            up_copy(dist).wait_recv()
+            value = value + up_in[dist].astype(F32)
+        return value
+
+    def gather_down(level, value):
+        for dist in range(level * stride + 1, min((level + 1) * stride, half - 1) + 1):
+            down_copy(dist).wait_recv()
+            value = value + down_in[dist].astype(F32)
+        return value
+
+    fill(levels - 1)
+    for level in range(levels - 1, 0, -1):
+        fill(level - 1)
+        dist = level * stride
+        send_up(dist, gather_up(level, chip_part(dist)))
+        send_down(dist, gather_down(level, chip_part(-dist)))
 
     own = products[slot_of(half - 1, core)] + from_sib[half - 1].astype(F32)
-    own = own + bias[...]
-    down_copy(half - 2).wait_recv()
-    own = own + down[half - 1].astype(F32)
-    up_copy(half - 1).wait_recv()
-    preact = own + up[half].astype(F32)
+    preact = gather_up(0, gather_down(0, own + bias[...]))
     hidden, slopes = gelu_parts(preact)
     grad_preact = cotangent[...] * slopes
     grads[core, z] = grad_preact.astype(BF16)
 
-    def right_copy(step):
-        at = grads.at[core, (z + nz - step) % nz]
-        return remote(at, at, right_send, right_recv.at[step], right)
-
-    def left_copy(step):
-        at = grads.at[core, (z + step) % nz]
-        return remote(at, at, left_send, left_recv.at[step], left)
+    def right_copy(level, hop):
+        at = grads.at[core, (z + nz - level * stride) % nz]
+        sem = right_recv.at[level * stride + hop]
+        return remote(at, at, right_send, sem, above(hop))
+
+    def left_copy(level, hop):
+        at = grads.at[core, (z + level * stride) % nz]
+        sem = left_recv.at[level * stride + hop]
+        return remote(at, at, left_send, sem, below(hop))
 
     def pass_copy(at_z):
         at = grads.at[core, at_z]
         return remote(at, at, pass_send, pass_recv, sibling)
 
-    right_copy(0).start()
-    left_copy(0).start()
+    def from_left(dist):
+        at = (z + nz - dist) % nz
+        settle(grads.at[core, at], right_recv.at[dist])
+        return at
+
+    def from_right(dist):
+        at = (z + dist) % nz
+        settle(grads.at[core, at], left_recv.at[dist])
+        return at
+
+    right_copy(0, stride).start()
+    left_copy(0, stride).start()
+    for hop in range(stride - 1, 0, -1):
+        right_copy(0, hop).start()
+        left_copy(0, hop).start()
     pass_copy(z).start()
     hidden_out[...] = hidden
     rows_dev, width_out = grad_preact.shape
@@ -319,27 +369,22 @@
     features_t[...] = features[...].T
 
 
-    @pl.loop(0, half)
-    def _(step):
-        from_left = (z + nz - 1 - step) % nz
-        right_copy(step).wait_recv()
-
-        @pl.when(step < half - 1)
-        def _():
-            right_copy(step + 1).start()
-
-        pass_copy(from_left).start()
-
-        @pl.when(step < half - 1)
-        def _():
-            from_right = (z + 1 + step) % nz
-            left_copy(step).wait_recv()
-
-            @pl.when(step < half - 2)
-            def _():
-                left_copy(step + 1).start()
-
-            pass_copy(from_right).start()
+    for level in range(1, levels + 1):
+        relayed = [from_left(level * stride)]
+        if level < levels:
+            right_copy(level, stride).start()
+            relayed.append(from_right(level * stride))
+            if level < levels - 1:
+                left_copy(level, stride).start()
+            for hop in range(stride - 1, 0, -1):
+                right_copy(level, hop).start()
+                left_copy(level, hop).start()
+        for at in relayed:
+            pass_copy(at).start()
+        for hop in range(1, stride):
+            dist = (level - 1) * stride + hop
+            pass_copy(from_left(dist)).start()
+            pass_copy(from_right(dist)).start()
 
     settle(grads.at[1 - core], pass_recv)
 
@@ -469,8 +514,8 @@
     for part in range(parts):
         for copy in sib_copies(part):
             copy.wait_send()
-    settle(up.at[pl.ds(0, half)], up_send)
-    settle(down.at[pl.ds(0, half - 1)], down_send)
+    settle(up.at[pl.ds(1, half)], up_send)
+    settle(down.at[pl.ds(1, half - 1)], down_send)
     settle(grads.at[0, pl.ds(0, half)], right_send)
     settle(grads.at[0, pl.ds(0, half - 1)], left_send)
     settle(grads.at[0], pass_send)
@@ -500,11 +545,9 @@
     rows_dev, f_in = features.shape
     f_out = weight.shape[1]
     nz = n_col // 2
-    half = nz // 2
-    near_n = math.gcd(8, nz) if nz >= 16 else 2
-    far_n = nz // near_n
+    half, stride, levels, near_n, far_n = plan(nz)
     n_plane = 2 * n_row
-    parts = min(4, half)
+    parts = levels
     nodes = rows_dev * n_row * n_col
     chunk = f_in // n_plane
     assert chunk == 8 and rows_dev == tile
@@ -519,9 +562,13 @@
             jax.ShapeDtypeStruct((n_plane, chunk, f_out), F32),
             jax.ShapeDtypeStruct((1, f_out), F32),
         ),
-        in_specs=[smem, smem, vmem, vmem, vmem, vmem, pl.BlockSpec(memory_space=pl.ANY)],
+        in_specs=[smem, smem] + [pl.BlockSpec(memory_space=pl.ANY)] * 5,
         out_specs=(vmem, vmem, vmem, vmem),
         scratch_shapes=[
+            pltpu.VMEM(features.shape, F32),
+            pltpu.VMEM(weight.shape, F32),
+            pltpu.VMEM((1, f_out), F32),
+            pltpu.VMEM(cotangent.shape, F32),
             pltpu.VMEM((slots, tile, tile), BF16),
             pltpu.VMEM((slots, tile, tile), BF16),
             pltpu.VMEM((f_in, rows_dev), F32),
@@ -531,7 +578,9 @@
             pltpu.VMEM((nz, tile, f_out), BF16),
             pltpu.VMEM((nz, tile, f_out), BF16),
             pltpu.VMEM((half + 1, tile, f_out), BF16),
-            pltpu.VMEM((half, tile, f_out), BF16),
+            pltpu.VMEM((half + 1, tile, f_out), BF16),
+            pltpu.VMEM((half + 1, tile, f_out), BF16),
+            pltpu.VMEM((half + 1, tile, f_out), BF16),
             pltpu.VMEM((2, nz, tile, f_out), BF16),
             pltpu.VMEM((n_row, tile, f_out), BF16),
             pltpu.VMEM((n_row, tile, f_out), BF16),
@@ -544,19 +593,19 @@
             pltpu.SMEM((slots,), jnp.int32),
             pltpu.SMEM((n_col,), jnp.int32),
             pltpu.SMEM((n_row,), jnp.int32),
-            dma,
+            dma((5,)),
             dma((n_row,)),
             dma((n_row,)),
             dma((2 * parts,)),
             dma((2 * parts,)),
             dma,
-            dma((half,)),
+            dma((half + 1,)),
             dma,
-            dma((half,)),
+            dma((half + 1,)),
             dma,
-            dma((half,)),
+            dma((half + 1,)),
             dma,
-            dma((half,)),
+            dma((half + 1,)),
             dma,
             dma,
             dma((n_row,)),

time: 191 us -> 149 us (0.78)
  Pallas kernels: 182 us -> 141 us
    pallas_call x1, Pallas kernels: 182 us -> 141 us  [local(): pl.pallas_call(functools.partial(layer, n_row, nz, 1.0 / math.sqrt(nodes)...]
where the time goes in v2:
time: 149 us
  Pallas kernels  141 us (95%)
  local copies, waits for them, and re-layouts  6.8 us (5%)
    pallas_call x1, Pallas kernels, local(): pl.pallas_call(functools.partial(layer, n_row, nz, 1.0 / math.sqrt(nodes)...  141 us
    unnamed x16, local copies, waits for them, and re-layouts  6.8 us

profile of v2, /device:TPU:1, one launch (start us, length us, event | category | flops | bytes accessed | tf_op | source)
XLA Modules:
  0.0 149.0 jit_solution(11096302905086269430)
XLA Ops:
  1.3 0.0 copy-start.4
  1.3 0.0 copy-start.5
  1.3 0.6 copy-done.4
  1.9 0.0 copy-done.5
  2.0 0.0 copy-start
  2.0 1.0 copy-done
  3.0 0.0 copy-start.1
  3.0 0.9 copy-done.1
  3.9 0.0 copy-start.2
  3.9 0.9 copy-done.2
  4.8 0.0 copy-start.3
  4.8 0.8 copy-done.3
  5.6 140.9 %shard_map.102 = (f32[128,128]{1,0:T(8,128)S(1)}, f32[128,256]{1,0:T(8,128)S(1)}, f32[32,8,128]{2,1,0:T(8,128)S(1)}, f32[1,128]{1,0:T(1,128)S(1)}) custom-call(s32[16]{0:T(128)S(1)} %bitcast.9, s32[1]{0:T(128)} %bitcast.6.live, f32[128,256]{1,0:T(8,128)S(1)} %copy-done.1, f32[256,128]{1,0:T(8,128)S(1)} %copy-done.2, f32[1,128]{1,0:T(1,128)S(1)} %bitcast.10, ...), custom_call_target="tpu_custom_call" | custom-call | tf_op jit(solution)/shard_map/pallas_call | solution.py:557
  146.5 0.6 copy.16
  147.2 0.7 copy.17
  147.8 0.7 copy.18
  148.5 0.5 copy.19
Async XLA Ops:
  1.3 0.7 copy-start.4
  1.3 0.7 copy-start.5
  2.0 1.0 copy-start
  3.0 0.9 copy-start.1
  3.9 0.9 copy-start.2
  4.8 0.8 copy-start.3

commit v3 on v2

--- a/solution.py
+++ b/solution.py
@@ -17,6 +17,18 @@
     stride = 4 if half % 4 == 0 and half > 4 else 2
     near_n = 8 if nz % 8 == 0 and nz > 8 else 2
     return half, stride, half // stride, near_n, nz // near_n
+
+
+def plane_steps(n_row):
+    width = 4 if n_row % 4 == 0 else n_row
+    height = n_row // width
+
+    def hops(step):
+        down, across = step
+        return min(down, height - down) + min(across, width - across)
+
+    steps = [(down, across) for down in range(height) for across in range(width)]
+    return width, sorted(steps, key=hops, reverse=True)[:-1]
 
 
 def gelu_parts(values):
@@ -71,6 +83,8 @@
     load_sem,
     panel_send,
     panel_recv,
+    features_send,
+    features_recv,
     sib_send,
     sib_recv,
     up_send,
@@ -94,12 +108,13 @@
     total_send,
     total_recv,
 ):
-    slots = tiles.shape[0]
+    slots, tile = tiles.shape[0], tiles.shape[1]
     row, col = lax.axis_index("row"), lax.axis_index("col")
     z, core = col // 2, col % 2
     half, stride, levels, near_n, far_n = plan(nz)
     n_plane = 2 * n_row
     place = 2 * row + core
+    width_x, steps = plane_steps(n_row)
     group, spot = z // near_n, z % near_n
 
     def device(at_row, at_z, at_core):
@@ -130,11 +145,11 @@
         other = (place + step) % n_plane
         return device(other // 2, z, other % 2), other
 
-    def near_peer(step):
-        return device(row, group * near_n + (spot + step) % near_n, core)
-
-    def far_peer(step):
-        return device(row, (z + near_n * step) % nz, core)
+    def peer(step):
+        down, across = step
+        return (row // width_x + down) % (n_row // width_x) * width_x + (
+            row + across
+        ) % width_x
 
     barrier = pltpu.get_barrier_semaphore()
 
@@ -143,13 +158,13 @@
             barrier, inc=1, device_id=to, device_id_type=pl.DeviceIdType.MESH
         )
 
-    for hop in range(1, stride + 1):
+    for hop in range(stride, 0, -1):
         greet(above(hop))
         greet(below(hop))
 
-    @pl.loop(1, n_plane)
-    def _(step):
-        greet(plane(step)[0])
+    for step in steps:
+        greet(device(peer(step), z, core))
+    greet(sibling)
 
     loads = [
         pltpu.make_async_copy(src, dst, load_sem.at[at])
@@ -170,20 +185,19 @@
     panel[row] = jnp.dot(
         features[...], weight[...], precision=HIGHEST, preferred_element_type=F32
     ).astype(BF16)
-    pl.semaphore_wait(barrier, n_plane - 1 + 2 * stride)
-
-    def panel_copy(step):
+    pl.semaphore_wait(barrier, n_row + 2 * stride)
+
+    def panel_copy(at):
         return remote(
             panel.at[row],
             panel.at[row],
-            panel_send.at[step],
-            panel_recv.at[step],
-            device((row + step) % n_row, z, core),
-        )
-
-    @pl.loop(1, n_row)
-    def _(step):
-        panel_copy(step).start()
+            panel_send,
+            panel_recv,
+            device(peer(steps[at]), z, core),
+        )
+
+    for at in range(n_row - 1):
+        panel_copy(at).start()
 
     count = live[0]
     n_cols = n_row
@@ -227,9 +241,7 @@
     for load in loads[2:]:
         load.wait()
 
-    @pl.loop(1, n_row)
-    def _(step):
-        panel_copy(step).wait_recv()
+    settle(panel.at[pl.ds(0, n_row - 1)], panel_recv)
 
     for slot in range(slots):
         products[slot] = jnp.dot(
@@ -249,7 +261,7 @@
             yield remote(
                 to_sib.at[pl.ds(first, width)],
                 from_sib.at[pl.ds(first, width)],
-                sib_send.at[2 * part + end],
+                sib_send,
                 sib_recv.at[2 * part + end],
                 sibling,
             )
@@ -312,11 +324,31 @@
         return value
 
     fill(levels - 1)
+    fill(levels - 2)
+
+    features_t[:, pl.ds(pl.multiple_of(row * tile, tile), tile)] = (
+        features[...].T.astype(BF16)
+    )
+
+    def features_copy(at):
+        mine = features_t.at[:, pl.ds(pl.multiple_of(row * tile, tile), tile)]
+        return remote(
+            mine,
+            mine,
+            features_send,
+            features_recv,
+            device(peer(steps[at]), z, core),
+        )
+
+    for at in range(n_row - 1):
+        features_copy(at).start()
+
     for level in range(levels - 1, 0, -1):
-        fill(level - 1)
         dist = level * stride
         send_up(dist, gather_up(level, chip_part(dist)))
         send_down(dist, gather_down(level, chip_part(-dist)))
+        if level > 1:
+            fill(level - 2)
 
     own = products[slot_of(half - 1, core)] + from_sib[half - 1].astype(F32)
     preact = gather_up(0, gather_down(0, own + bias[...]))
@@ -350,10 +382,14 @@
 
     right_copy(0, stride).start()
     left_copy(0, stride).start()
-    for hop in range(stride - 1, 0, -1):
-        right_copy(0, hop).start()
-        left_copy(0, hop).start()
     pass_copy(z).start()
+
+    def serve_between(level):
+        for hop in range(stride - 1, 0, -1):
+            right_copy(level, hop).start()
+            left_copy(level, hop).start()
+
+    serve_between(0)
     hidden_out[...] = hidden
     rows_dev, width_out = grad_preact.shape
     bias_term = jnp.sum(grad_preact.reshape(rows_dev // 8, 8, width_out), axis=0)
@@ -365,8 +401,6 @@
     @pl.loop(0, slots)
     def _(slot):
         tiles_t[slot] = tiles[slot].T
-
-    features_t[...] = features[...].T
 
 
     for level in range(1, levels + 1):
@@ -376,11 +410,10 @@
             relayed.append(from_right(level * stride))
             if level < levels - 1:
                 left_copy(level, stride).start()
-            for hop in range(stride - 1, 0, -1):
-                right_copy(level, hop).start()
-                left_copy(level, hop).start()
         for at in relayed:
             pass_copy(at).start()
+        if level < levels:
+            serve_between(level)
         for hop in range(1, stride):
             dist = (level - 1) * stride + hop
             pass_copy(from_left(dist)).start()
@@ -400,33 +433,12 @@
     def _(slot):
         products[slot] = products[slot] + products[prev_col[slot]]
 
-    def back_copy(step):
-        to = (row + step) % n_row
-        return remote(
-            back.at[step],
-            back_in.at[step],
-            back_send.at[step],
-            back_recv.at[step],
-            device(to, z, core),
-        )
-
-    @pl.loop(1, n_row)
-    def _(step):
-        back[step] = products[last_col[(row + step) % n_row]].astype(BF16)
-        back_copy(step).start()
-
-    products[slots] = products[last_col[row]].astype(BF16).astype(F32)
-
-    @pl.loop(1, n_row)
-    def _(step):
-        back_copy(step).wait_recv()
-        products[slots] = products[slots] + back_in[step].astype(F32)
-
-    grad_product = products[slots]
-
-    weight_term = jnp.dot(
-        features_t[...], grad_product, precision=HIGHEST, preferred_element_type=F32
-    )
+    for at in range(n_row):
+        back[at * tile : (at + 1) * tile] = products[last_col[at]].astype(BF16)
+
+    features_but_own = features_t.at[:, pl.ds(0, (n_row - 1) * tile)]
+    settle(features_but_own, features_recv)
+    weight_term = jnp.dot(features_t[...], back[...], preferred_element_type=F32)
     for at in range(n_plane):
         terms[at, 0:8] = weight_term[8 * at : 8 * at + 8]
 
@@ -435,8 +447,8 @@
         return remote(
             terms.at[other],
             terms_in.at[place],
-            terms_send.at[step],
-            terms_recv.at[step],
+            terms_send,
+            terms_recv,
             to,
         )
 
@@ -444,6 +456,47 @@
     def _(step):
         terms_copy(step).start()
 
+    def back_copy(at):
+        to = peer(steps[at])
+        return remote(
+            back.at[pl.ds(pl.multiple_of(to * tile, tile), tile)],
+            back_in.at[at],
+            back_send,
+            back_recv,
+            device(to, z, core),
+        )
+
+    terms_in[place] = terms[place]
+
+    settle(terms_in.at[pl.ds(0, n_plane - 1)], terms_recv)
+    near[spot] = lax.fori_loop(
+        1, n_plane, lambda at, so_far: so_far + terms_in[at], terms_in[0]
+    )
+
+    def near_copy(step):
+        at = near.at[spot]
+        to = device(row, group * near_n + (spot + step) % near_n, core)
+        return remote(at, at, near_send, near_recv, to)
+
+    def far_copy(step):
+        at = far.at[group]
+        to = above(near_n * step)
+        return remote(at, at, far_send, far_recv, to)
+
+    for step in range(1, near_n):
+        near_copy(step).start()
+    for at in range(n_row - 1):
+        back_copy(at).start()
+    settle(near.at[pl.ds(0, near_n - 1)], near_recv)
+    far[group] = sum((near[at] for at in range(1, near_n)), near[0])
+    for step in range(1, far_n):
+        far_copy(step).start()
+
+    mine = back[pl.ds(pl.multiple_of(row * tile, tile), tile)]
+    grad_product = mine.astype(F32)
+    settle(back_in.at[pl.ds(0, n_row - 1)], back_recv)
+    for at in range(n_row - 1):
+        grad_product = grad_product + back_in[at].astype(F32)
     grad_features_out[...] = lax.dot_general(
         grad_product,
         weight[...],
@@ -451,43 +504,8 @@
         precision=HIGHEST,
         preferred_element_type=F32,
     )
-    terms_in[place] = terms[place]
-
-    @pl.loop(1, n_plane)
-    def _(step):
-        terms_copy(step).wait_recv()
-
-    near[spot] = lax.fori_loop(
-        1, n_plane, lambda at, so_far: so_far + terms_in[at], terms_in[0]
-    )
-
-    def near_copy(step):
-        return remote(
-            near.at[spot],
-            near.at[spot],
-            near_send.at[step],
-            near_recv.at[step],
-            near_peer(step),
-        )
-
-    def far_copy(step):
-        return remote(
-            far.at[group],
-            far.at[group],
-            far_send.at[step],
-            far_recv.at[step],
-            far_peer(step),
-        )
-
-    for step in range(1, near_n):
-        near_copy(step).start()
-    for step in range(1, near_n):
-        near_copy(step).wait_recv()
-    far[group] = sum((near[at] for at in range(1, near_n)), near[0])
-    for step in range(1, far_n):
-        far_copy(step).start()
-    for step in range(1, far_n):
-        far_copy(step).wait_recv()
+
+    settle(far.at[pl.ds(0, far_n - 1)], far_recv)
     summed = sum((far[at] for at in range(1, far_n)), far[0]) * scaling
     total[place] = summed[0:8]
 
@@ -495,8 +513,8 @@
         return remote(
             total.at[place],
             total.at[place],
-            total_send.at[step],
-            total_recv.at[step],
+            total_send,
+            total_recv,
             plane(step)[0],
         )
 
@@ -506,38 +524,21 @@
 
     grad_bias_out[...] = jnp.sum(summed[8:16], axis=0, keepdims=True)
 
-    @pl.loop(1, n_row)
-    def _(step):
-        panel_copy(step).wait_send()
-        back_copy(step).wait_send()
-
-    for part in range(parts):
-        for copy in sib_copies(part):
-            copy.wait_send()
+    settle(panel.at[pl.ds(0, n_row - 1)], panel_send)
+    settle(features_but_own, features_send)
+    settle(back_in.at[pl.ds(0, n_row - 1)], back_send)
+    settle(to_sib, sib_send)
     settle(up.at[pl.ds(1, half)], up_send)
     settle(down.at[pl.ds(1, half - 1)], down_send)
     settle(grads.at[0, pl.ds(0, half)], right_send)
     settle(grads.at[0, pl.ds(0, half - 1)], left_send)
     settle(grads.at[0], pass_send)
-
-    @pl.loop(1, n_plane)
-    def _(step):
-        terms_copy(step).wait_send()
-
-    for step in range(1, near_n):
-        near_copy(step).wait_send()
-    for step in range(1, far_n):
-        far_copy(step).wait_send()
-
-    @pl.loop(1, n_plane)
-    def _(step):
-        total_copy(step).wait_recv()
-
+    settle(terms_in.at[pl.ds(0, n_plane - 1)], terms_send)
+    settle(near.at[pl.ds(0, near_n - 1)], near_send)
+    settle(far.at[pl.ds(0, far_n - 1)], far_send)
+    settle(total.at[pl.ds(0, n_plane - 1)], total_send)
+    settle(total.at[pl.ds(0, n_plane - 1)], total_recv)
     grad_weight_out[...] = total[...]
-
-    @pl.loop(1, n_plane)
-    def _(step):
-        total_copy(step).wait_send()
 
 
 def local(n_row, n_col, features, weight, bias, tiles, where, live, cotangent):
@@ -562,7 +563,7 @@
             jax.ShapeDtypeStruct((n_plane, chunk, f_out), F32),
             jax.ShapeDtypeStruct((1, f_out), F32),
         ),
-        in_specs=[smem, smem] + [pl.BlockSpec(memory_space=pl.ANY)] * 5,
+        in_specs=[smem, smem] + [pl.BlockSpec(memory_space=pltpu.HBM)] * 5,
         out_specs=(vmem, vmem, vmem, vmem),
         scratch_shapes=[
             pltpu.VMEM(features.shape, F32),
@@ -571,7 +572,7 @@
             pltpu.VMEM(cotangent.shape, F32),
             pltpu.VMEM((slots, tile, tile), BF16),
             pltpu.VMEM((slots, tile, tile), BF16),
-            pltpu.VMEM((f_in, rows_dev), F32),
+            pltpu.VMEM((f_in, n_row * rows_dev), BF16),
             pltpu.VMEM((n_row, tile, f_out), BF16),
             pltpu.VMEM((slots + 1, tile, f_out), F32),
             pltpu.VMEM((slots + 1, tile, f_out), BF16),
@@ -582,7 +583,7 @@
             pltpu.VMEM((half + 1, tile, f_out), BF16),
             pltpu.VMEM((half + 1, tile, f_out), BF16),
             pltpu.VMEM((2, nz, tile, f_out), BF16),
-            pltpu.VMEM((n_row, tile, f_out), BF16),
+            pltpu.VMEM((n_row * tile, f_out), BF16),
             pltpu.VMEM((n_row, tile, f_out), BF16),
             pltpu.VMEM((n_plane, 2 * chunk, f_out), F32),
             pltpu.VMEM((n_plane, 2 * chunk, f_out), F32),
@@ -594,10 +595,12 @@
             pltpu.SMEM((n_col,), jnp.int32),
             pltpu.SMEM((n_row,), jnp.int32),
             dma((5,)),
-            dma((n_row,)),
-            dma((n_row,)),
+            dma,
+            dma,
+            dma,
+            dma,
+            dma,
             dma((2 * parts,)),
-            dma((2 * parts,)),
             dma,
             dma((half + 1,)),
             dma,
@@ -608,19 +611,19 @@
             dma((half + 1,)),
             dma,
             dma,
-            dma((n_row,)),
-            dma((n_row,)),
-            dma((n_plane,)),
-            dma((n_plane,)),
-            dma((near_n,)),
-            dma((near_n,)),
-            dma((far_n,)),
-            dma((far_n,)),
-            dma((n_plane,)),
-            dma((n_plane,)),
+            dma,
+            dma,
+            dma,
+            dma,
+            dma,
+            dma,
+            dma,
+            dma,
+            dma,
+            dma,
         ],
         compiler_params=pltpu.CompilerParams(
-            collective_id=0, has_side_effects=True, vmem_limit_bytes=48 * 1024 * 1024
+            collective_id=0, has_side_effects=True, vmem_limit_bytes=56 * 1024 * 1024
         ),
     )(
         where.reshape(slots),

time: 149 us -> 134 us (0.90)
  Pallas kernels: 141 us -> 129 us
  local copies, waits for them, and re-layouts: 6.8 us -> 3.64 us
    pallas_call x1, Pallas kernels: 141 us -> 129 us  [local(): pl.pallas_call(functools.partial(layer, n_row, nz, 1.0 / math.sqrt(nodes)...]
    unnamed x16 -> x10, local copies, waits for them, and re-layouts: 6.8 us -> 3.64 us
where the time goes in v3:
time: 134 us
  Pallas kernels  129 us (96%)
  local copies, waits for them, and re-layouts  3.64 us (3%)
    pallas_call x1, Pallas kernels, local(): pl.pallas_call(functools.partial(layer, n_row, nz, 1.0 / math.sqrt(nodes)...  129 us
    unnamed x10, local copies, waits for them, and re-layouts  3.64 us

profile of v3, /device:TPU:1, one launch (start us, length us, event | category | flops | bytes accessed | tf_op | source)
XLA Modules:
  0.0 134.0 jit_solution(15775826149495993221)
XLA Ops:
  1.3 129.1 %shard_map.102 = (f32[128,128]{1,0:T(8,128)}, f32[128,256]{1,0:T(8,128)}, f32[32,8,128]{2,1,0:T(8,128)}, f32[1,128]{1,0:T(1,128)}) custom-call(s32[16]{0:T(128)} %bitcast.9, s32[1]{0:T(128)} %bitcast.6.live, f32[128,256]{1,0:T(8,128)} %features_hbm.1, f32[256,128]{1,0:T(8,128)} %weight_hbm.1, f32[1,128]{1,0:T(1,128)} %bitcast.10, f32[128,128]{1,0:T(8,128)} %cotangent_hbm.1, ...), custom_call_target="tpu_custom_call" | custom-call | tf_op jit(solution)/shard_map/pallas_call | solution.py:558
  130.4 0.0 copy-start.1
  130.4 1.5 %copy.16 = f32[128,128]{1,0:T(8,128)} copy(f32[128,128]{1,0:T(8,128)} %get-tuple-element.16) | data formatting | bytes 131072
  131.9 0.0 copy-done.1
  131.9 0.0 copy-start
  131.9 0.7 copy.17
  132.5 0.3 copy-done
  132.8 0.0 copy-start.2
  132.8 0.7 copy.18
  133.5 0.0 copy-done.2
  133.5 0.5 copy.19
Async XLA Ops:
  130.4 1.5 %copy-start.1 = (f32[128,256]{1,0:T(8,128)S(1)}, f32[128,256]{1,0:T(8,128)}, u32[]{:S(2)}) copy-start(f32[128,256]{1,0:T(8,128)} %get-tuple-element.17) | copy-start | bytes 393220
  131.9 1.0 copy-start
  132.8 0.7 copy-start.2
